TPU v7x, 256 devices: a whole 4x4x8 slice. The times are simulated.
256 devices in a mesh: leaf: 64 (over z, x, core), mode: 4 (over y).
Axes of the slice: x: 4, y: 4, z: 8, core: 2. Of those that a mesh axis runs over, the one named last changes fastest.
Arguments:
- leaf_sizes: int32 [256], P('leaf'), may hold values from 1 to 128, 24576 in all
- leaf_stiffness: float32 [32768], P('leaf'), may hold values from 1 to 8
- coupling: float32 [3, 32768, 512], P(None, 'leaf', 'mode'), may hold values from -0.25 to 0.25
- omega_root: float32 [512], P('leaf'), may hold values from 1 to 8
- omega_mid: float32 [1024], P('leaf'), may hold values from 1 to 8
- omega_low: float32 [2048], P('leaf'), may hold values from 1 to 8
- start_leaf: float32 [256, 32768], P('mode', 'leaf'), may hold values from -6 to 6
- start_root: float32 [256, 512], P('mode', 'leaf'), may hold values from -6 to 6
- start_mid: float32 [256, 1024], P('mode', 'leaf'), may hold values from -6 to 6
- start_low: float32 [256, 2048], P('mode', 'leaf'), may hold values from -6 to 6
Outputs:
- vectors_leaf: float32 [256, 32768], P('mode', 'leaf')
- vectors_root: float32 [256, 512], P('mode', 'leaf')
- vectors_mid: float32 [256, 1024], P('mode', 'leaf')
- vectors_low: float32 [256, 2048], P('mode', 'leaf')
- mass_root: float32 [512, 512], P('leaf', 'mode')
- mass_mid: float32 [1024, 512], P('leaf', 'mode')
- mass_low: float32 [2048, 512], P('leaf', 'mode')
Inputs may be any that keep to these rules, and one draw needn't show every extreme that they name: leaf_sizes[l] counts the live modal coordinates of substructure l; they sum to 24576 and the largest is 128.
All inputs are finite; a program needn't handle non-finite values. No bound on the sum of `leaf_sizes` on one device may be relied on, other than what follows from the above.
Results may differ from a plain program's by a relative error of at most 0.00013.
Values sent between devices are 32-bit elements; how exact they have to be, the bound alone decides.
A program may use at most 64 MiB of HBM per device.

v0:
```python
import jax
import jax.numpy as jnp
from jax import lax
from jax.sharding import PartitionSpec as P

ITERS = 3


def place_rows(block_values, group_number, groups, leaf_count):
    selector = (jnp.arange(groups) == group_number).astype(jnp.float32)
    placed = selector[:, None, None] * block_values[None]
    return placed.reshape(
        leaf_count, groups * block_values.shape[0] // leaf_count, block_values.shape[1]
    )


def place_columns(values, group_number, groups, leaf_count):
    selector = (jnp.arange(groups) == group_number).astype(jnp.float32)
    placed = values[:, None, :] * selector[None, :, None]
    return placed.reshape(values.shape[0], leaf_count, groups * values.shape[1] // leaf_count)


def local(
    leaf_sizes,
    leaf_stiffness,
    coupling,
    omega_root,
    omega_mid,
    omega_low,
    start_leaf,
    start_root,
    start_mid,
    start_low,
):
    precise = lax.Precision.HIGHEST
    leaf_count = lax.axis_size("leaf")
    leaf_index = lax.axis_index("leaf")
    mode_index = lax.axis_index("mode")
    modal_rows = leaf_stiffness.shape[0]
    local_leaves = leaf_sizes.shape[0]
    leaf_width = modal_rows // local_leaves
    column_count = start_leaf.shape[0]
    column_share = coupling.shape[2]
    interface_width = column_share * lax.axis_size("mode")
    span_sizes = [omega_root.shape[0], omega_mid.shape[0], omega_low.shape[0]]
    span_total = sum(span_sizes)
    offsets = [0, span_sizes[0], span_sizes[0] + span_sizes[1], span_total]
    group_index = [leaf_index // (leaf_count >> tree_level) for tree_level in range(3)]
    live_mask = (
        (jnp.arange(leaf_width)[None, :] < leaf_sizes[:, None])
        .astype(jnp.float32)
        .reshape(modal_rows)
    )
    inverse = live_mask / leaf_stiffness
    full_coupling = lax.all_gather(coupling, "mode", axis=2, tiled=True)
    projected = jnp.einsum(
        "hli,hlj->hij",
        full_coupling * (inverse * inverse)[None, :, None],
        coupling,
        precision=precise,
    )
    mass_pieces = [
        place_rows(projected[tree_level], group_index[tree_level], 2**tree_level, leaf_count)
        for tree_level in range(3)
    ]
    mass_stack = jnp.concatenate(mass_pieces, axis=1).reshape(leaf_count * span_total, column_share)
    mass_own = lax.psum_scatter(mass_stack, "leaf", scatter_dimension=0, tiled=True)
    col_ids = mode_index * column_share + jnp.arange(column_share)
    mass_parts = []
    for tree_level in range(3):
        row_ids = leaf_index * span_sizes[tree_level] + jnp.arange(span_sizes[tree_level])
        unit_block = ((row_ids % interface_width)[:, None] == col_ids[None, :]).astype(jnp.float32)
        mass_parts.append(mass_own[offsets[tree_level] : offsets[tree_level + 1]] + unit_block)
    omega_own = jnp.concatenate([omega_root, omega_mid, omega_low])
    leaf_values = start_leaf * live_mask[None, :]
    interface_own = jnp.concatenate([start_root, start_mid, start_low], axis=1)
    rows_all = leaf_count * modal_rows + 7 * interface_width
    for sweep_index in range(ITERS):
        gathered = lax.all_gather(interface_own, "leaf", axis=1, tiled=True).reshape(
            column_count, leaf_count, span_total
        )
        current = []
        for tree_level in range(3):
            whole_level = gathered[:, :, offsets[tree_level] : offsets[tree_level + 1]].reshape(
                column_count, -1
            )
            current.append(
                lax.dynamic_slice_in_dim(
                    whole_level, group_index[tree_level] * interface_width, interface_width, 1
                )
            )
        stacked = jnp.stack(current)
        coupled = jnp.einsum("hpi,hli->pl", stacked, full_coupling, precision=precise)
        modal_mass = live_mask[None, :] * leaf_values - inverse[None, :] * coupled
        modal_next = modal_mass * inverse[None, :]
        interface_terms = jnp.einsum("pl,hli->hpi", modal_next, full_coupling, precision=precise)
        pieces = [
            place_columns(
                interface_terms[tree_level], group_index[tree_level], 2**tree_level, leaf_count
            )
            for tree_level in range(3)
        ]
        padded_terms = jnp.concatenate(pieces, axis=2).reshape(
            column_count, leaf_count * span_total
        )
        summed = lax.psum_scatter(padded_terms, "leaf", scatter_dimension=1, tiled=True)
        interface_mass = interface_own - summed
        interface_next = interface_mass / omega_own[None, :]
        next_rows = jnp.concatenate([modal_next, interface_next], axis=1)
        mass_rows = jnp.concatenate([modal_mass, interface_mass], axis=1)
        next_full = lax.all_gather(next_rows, "mode", axis=0, tiled=True)
        gram_part = jnp.dot(next_full, mass_rows.T, precision=precise) / rows_all
        gram_leaf = lax.psum(gram_part, "leaf")
        gram_matrix = lax.all_gather(gram_leaf, "mode", axis=1, tiled=True)
        gram_matrix = 0.5 * (gram_matrix + gram_matrix.T)
        lower_factor = jnp.linalg.cholesky(gram_matrix)
        solved = jax.scipy.linalg.solve_triangular(lower_factor, next_full, lower=True)
        own_rows = lax.dynamic_slice_in_dim(solved, mode_index * column_count, column_count, 0)
        leaf_values = own_rows[:, :modal_rows]
        interface_own = own_rows[:, modal_rows:]
    return (
        leaf_values,
        interface_own[:, offsets[0] : offsets[1]],
        interface_own[:, offsets[1] : offsets[2]],
        interface_own[:, offsets[2] : offsets[3]],
        mass_parts[0],
        mass_parts[1],
        mass_parts[2],
    )


def solution(mesh):
    placed = (
        P("leaf"),
        P("leaf"),
        P(None, "leaf", "mode"),
        P("leaf"),
        P("leaf"),
        P("leaf"),
        P("mode", "leaf"),
        P("mode", "leaf"),
        P("mode", "leaf"),
        P("mode", "leaf"),
    )
    return jax.shard_map(
        local,
        mesh=mesh,
        in_specs=placed,
        out_specs=(
            P("mode", "leaf"),
            P("mode", "leaf"),
            P("mode", "leaf"),
            P("mode", "leaf"),
            P("leaf", "mode"),
            P("leaf", "mode"),
            P("leaf", "mode"),
        ),
        check_vma=False,
    )
```

profile of v0, /device:TPU:1, one launch (start us, length us, event | category | flops | bytes accessed | tf_op | source)
XLA Modules:
  0.0 1610.8 jit_solution(15518466064490603506)
XLA Ops:
  11.0 55.2 %all_gather.30 = f32[64,3584]{0,1:T(8,128)S(1)} all-gather(f32[64,56]{0,1:T(8,128)S(1)} %copy.96), channel_id=1, replica_groups=mesh['leaf'=64,'mode'=4] {'leaf'}, dimensions={1}, use_global_device_ids=true | all-gather | bytes 931840 | tf_op jit(solution)/shard_map/all_gather | solution.py:79
  88.9 179.7 %all-reduce.17.cloned.1.call-done = f32[64,3584]{1,0:T(8,128)} async-done(((f32[64,3584]{1,0:T(8,128)}), f32[64,3584]{1,0:T(8,128)}) %all-reduce.17.cloned.1.call-update) | async-done | bytes 917520
  269.6 10.6 all_gather.32
  283.0 170.1 %all-reduce.13.cloned.1.call-done = f32[256,64]{0,1:T(8,128)} async-done(((f32[256,64]{0,1:T(8,128)}), f32[256,64]{0,1:T(8,128)}) %all-reduce.13.cloned.1.call-update) | async-done | bytes 65552 | tf_op jit(solution)/shard_map/psum | solution.py:113
  453.1 10.6 all_gather.33
  468.9 11.7 cholesky.172
  493.2 11.7 cholesky.189
  516.3 20.3 %custom-call.16 = f32[2,128,128]{1,2,0:T(8,128)} custom-call(f32[2,128,128]{2,1,0:T(8,128)S(1)} %get-tuple-element.29), custom_call_target="InvertDiagBlocksLowerTriangular" | custom-call | tf_op jit(solution)/shard_map/jit(_solve_triangular)/triangular_solve | solution.py:117
  544.6 52.6 %all_gather.34 = f32[64,3584]{0,1:T(8,128)S(1)} all-gather(f32[64,56]{0,1:T(8,128)S(1)} %copy.113), channel_id=1, replica_groups=mesh['leaf'=64,'mode'=4] {'leaf'}, dimensions={1}, use_global_device_ids=true | all-gather | bytes 931840 | tf_op jit(solution)/shard_map/all_gather | solution.py:79
  627.9 171.0 %all-reduce.19.cloned.1.call-done = f32[64,3584]{1,0:T(8,128)} async-done(((f32[64,3584]{1,0:T(8,128)}), f32[64,3584]{1,0:T(8,128)}) %all-reduce.19.cloned.1.call-update) | async-done | bytes 917520
  799.9 10.6 all_gather.35
  814.7 168.6 %all-reduce.15.cloned.1.call-done = f32[256,64]{0,1:T(8,128)} async-done(((f32[256,64]{0,1:T(8,128)}), f32[256,64]{0,1:T(8,128)}) %all-reduce.15.cloned.1.call-update) | async-done | bytes 65552 | tf_op jit(solution)/shard_map/psum | solution.py:113
  983.3 10.6 all_gather.36
  999.1 11.7 cholesky.206
  1023.4 11.7 cholesky.223
  1045.8 20.3 %custom-call.18 = f32[2,128,128]{1,2,0:T(8,128)} custom-call(f32[2,128,128]{2,1,0:T(8,128)S(1)} %get-tuple-element.30), custom_call_target="InvertDiagBlocksLowerTriangular" | custom-call | tf_op jit(solution)/shard_map/jit(_solve_triangular)/triangular_solve | solution.py:117
  1074.2 52.6 %all_gather.37 = f32[64,3584]{0,1:T(8,128)S(1)} all-gather(f32[64,56]{0,1:T(8,128)S(1)} %copy.130), channel_id=1, replica_groups=mesh['leaf'=64,'mode'=4] {'leaf'}, dimensions={1}, use_global_device_ids=true | all-gather | bytes 931840 | tf_op jit(solution)/shard_map/all_gather | solution.py:79
  1145.2 175.9 %all-reduce.21.cloned.1.call-done = f32[64,3584]{1,0:T(8,128)} async-done(((f32[64,3584]{1,0:T(8,128)}), f32[64,3584]{1,0:T(8,128)}) %all-reduce.21.cloned.1.call-update) | async-done | bytes 917520
  1322.0 10.6 all_gather.38
  1334.1 189.9 %all-reduce.23.cloned.1.call-done = (f32[256,64]{0,1:T(8,128)}, f32[3584,128]{1,0:T(8,128)}) async-done(((f32[256,64]{0,1:T(8,128)}, f32[3584,128]{1,0:T(8,128)}), (f32[256,64]{0,1:T(8,128)}, f32[3584,128]{1,0:T(8,128)})) %all-reduce.23.cloned.1.call-update) | async-done | bytes 1900560 | tf_op jit(solution)/shard_map/psum | solution.py:113
  1524.0 10.1 all_gather.39
  1534.5 11.7 cholesky.240
  1556.5 11.7 cholesky.257
  1575.1 19.7 %custom-call.20 = f32[2,128,128]{1,2,0:T(8,128)S(1)} custom-call(f32[2,128,128]{2,1,0:T(8,128)S(1)} %get-tuple-element.31), custom_call_target="InvertDiagBlocksLowerTriangular" | custom-call | tf_op jit(solution)/shard_map/jit(_solve_triangular)/triangular_solve | solution.py:117
  (275 shorter events, 196.3 us)
Async XLA Ops:
  7.2 63.2 %all-gather.2.cloned.1.call-start = ((), (), s32[]{:S(2)}) async-start(), calls=%async_computation | async-start | bytes 3932160 | tf_op jit(solution)/shard_map/all_gather | solution.py:55
  7.9 260.7 %all-reduce.17.cloned.1.call-start = ((), (), s32[]{:S(2)}) async-start(), calls=%async_computation.3 | async-start | bytes 1835008
  66.4 3.3 copy-start.30
  66.4 3.3 copy-start.29
  70.4 5.8 copy-start
  84.4 4.4 copy-start.31
  84.4 4.4 copy-start.32
  84.4 4.4 copy-start.33
  84.4 184.2 %copy-start.20 = (f32[64,16]{1,0:T(8,128)S(1)}, f32[64,16]{1,0:T(8,128)}, u32[]{:S(2)}) copy-start(f32[64,16]{1,0:T(8,128)} %copy-done.19) | copy-start | bytes 12292
  84.4 184.2 %copy-start.22 = (f32[64,8]{1,0:T(8,128)S(1)}, f32[64,8]{1,0:T(8,128)}, u32[]{:S(2)}) copy-start(f32[64,8]{1,0:T(8,128)} %copy-done.21) | copy-start | bytes 6148
  84.4 184.2 %copy-start.24 = (f32[64,32]{1,0:T(8,128)S(1)}, f32[64,32]{1,0:T(8,128)}, u32[]{:S(2)}) copy-start(f32[64,32]{1,0:T(8,128)} %copy-done.23) | copy-start | bytes 24580
  87.4 193.6 %copy-start.17 = (f32[64,512]{1,0:T(8,128)S(1)}, f32[64,512]{1,0:T(8,128)}, u32[]{:S(2)}) copy-start(f32[64,512]{1,0:T(8,128)} %get-tuple-element.118) | copy-start | bytes 393220
  87.4 365.7 %all-reduce.13.cloned.1.call-start = ((), (), s32[]{:S(2)}) async-start(), calls=%async_computation.1 | async-start | bytes 131072 | tf_op jit(solution)/shard_map/psum | solution.py:113
  88.9 377.5 %copy-start.25 = (f32[56]{0:T(128)}, f32[56]{0:T(128)S(1)}, u32[]{:S(2)}) copy-start(f32[56]{0:T(128)S(1)} %pad_maximum_fusion.8) | copy-start | bytes 676
  282.4 516.5 %all-reduce.19.cloned.1.call-start = ((), (), s32[]{:S(2)}) async-start(), calls=%async_computation.4 | async-start | bytes 1835008
  617.5 3.2 copy-start.28
  620.5 362.9 %all-reduce.15.cloned.1.call-start = ((), (), s32[]{:S(2)}) async-start(), calls=%async_computation.2 | async-start | bytes 131072 | tf_op jit(solution)/shard_map/psum | solution.py:113
  620.7 178.2 %copy-start.26 = (f32[56]{0:T(128)S(1)}, f32[56]{0:T(128)}, u32[]{:S(2)}) copy-start(f32[56]{0:T(128)} %copy-done.25) | copy-start | bytes 676
  620.7 190.6 %copy-start.18 = (f32[64,512]{1,0:T(8,128)S(1)}, f32[64,512]{1,0:T(8,128)}, u32[]{:S(2)}) copy-start(f32[64,512]{1,0:T(8,128)} %get-tuple-element.122) | copy-start | bytes 393220
  812.7 508.4 %all-reduce.21.cloned.1.call-start = ((), (), s32[]{:S(2)}) async-start(), calls=%async_computation.5 | async-start | bytes 1835008
  1035.1 3.2 copy-start.10
  1142.6 381.4 %all-reduce.23.cloned.1.call-start = ((), (), s32[]{:S(2)}) async-start(), calls=%async_computation.6 | async-start | bytes 3801088 | tf_op jit(solution)/shard_map/psum | solution.py:113
  1143.8 177.2 %copy-start.27 = (f32[56]{0:T(128)S(1)}, f32[56]{0:T(128)}, u32[]{:S(2)}) copy-start(f32[56]{0:T(128)} %copy-done.25) | copy-start | bytes 676
  1534.2 36.7 %copy-start.34 = (s32[2,2]{1,0:T(2,128)S(1)}, s32[2,2]{1,0:T(2,128)}, u32[]{:S(2)}) copy-start(s32[2,2]{1,0:T(2,128)} %get-tuple-element.301) | copy-start | bytes 52
  (19 other events, 21.0 us)
Sparse Core Ops, SparseCore 0:
  9.8 48.7 all-gather.1
  87.6 180.9 all-reduce.16
  282.5 170.5 all-reduce.12
  620.6 178.2 all-reduce.18
  812.8 170.4 all-reduce.14
  1142.8 178.2 all-reduce.20
  1334.1 189.8 all-reduce.22
where the time goes:
time: 1620 us; the launch traced here: 1610 us
  waiting for transfers between devices  1060 us (65%)
  blocking collectives  223 us (14%)
  other arithmetic  196 us (12%)
  local copies, waits for them, and re-layouts  64 us (4%)
  matrix products  49.6 us (3%)
  between operations  19.8 us (1%)
    psum x3, waiting for transfers between devices, local(): gram_leaf = lax.psum(gram_part, 'leaf')  529 us
    unnamed x10, waiting for transfers between devices  527 us
    all_gather x3, blocking collectives, local(): lax.all_gather(interface_own, 'leaf', axis=1, tiled=True)  160 us
    another operation x20, other arithmetic, local(): lower_factor = jnp.linalg.cholesky(gram_matrix)  105 us
    another operation x10, other arithmetic, local(): jax.scipy.linalg.solve_triangular(lower_factor, next_full, lower=True)  64.9 us
  transfers between devices with their start and end apart: 7, of which 6 were waited for; matrix products, arithmetic and copies ran while one was open for 1% of the time, Pallas kernels for 0%

commit v1 on v0

v1 whole, which is shorter than its diff:
```python
import functools
import jax
import jax.numpy as jnp
from jax import lax
from jax.experimental import pallas as pl
from jax.experimental.pallas import tpu as pltpu
from jax.sharding import PartitionSpec as P

ITERS = 3
ROWS = 36352.0
SCALE = 2.0**-12
MESH = pl.DeviceIdType.MESH
HI = lax.Precision.HIGHEST
F32 = jnp.float32
BF16 = jnp.bfloat16
NEAR_FIRST = ((0, 1), (0, 3), (1, 0), (0, 2), (1, 1), (1, 3), (1, 2))


def nt(a, b):
    return lax.dot_general(a, b, (((1,), (1,)), ((), ())), precision=HI, preferred_element_type=F32)


def nn(a, b):
    return lax.dot_general(a, b, (((1,), (0,)), ((), ())), precision=HI, preferred_element_type=F32)


def tn(a, b):
    return lax.dot_general(a, b, (((0,), (0,)), ((), ())), precision=HI, preferred_element_type=F32)


def halves(x):
    high = x.astype(BF16)
    return high, (x - high.astype(F32)).astype(BF16)


def nn16(a, b):
    return lax.dot_general(a, b, (((1,), (0,)), ((), ())), preferred_element_type=F32)


def nt16(a, b):
    return lax.dot_general(a, b, (((1,), (1,)), ((), ())), preferred_element_type=F32)


def root_row(q, n):
    return q * 128 + 8 * n


def mid_row(half, n):
    return 512 + half * 256 + 16 * n


def low_row(n):
    return 1024 + 32 * n


def remote(src, dst, send, recv, leaf, mode):
    return pltpu.make_async_remote_copy(
        src_ref=src,
        dst_ref=dst,
        send_sem=send,
        recv_sem=recv,
        device_id=(leaf, mode),
        device_id_type=MESH,
    )


def column(ref):
    n = ref.shape[1]
    r = lax.broadcasted_iota(jnp.int32, (n, n), 0)
    c = lax.broadcasted_iota(jnp.int32, (n, n), 1)
    spread = jnp.where(r == c, jnp.broadcast_to(ref[...], (n, n)), 0.0)
    return jnp.broadcast_to(jnp.sum(spread, axis=1, keepdims=True), (n, 64))


def sweeps_kernel(
    sizes_ref,
    stiff_in,
    coupling_ref,
    leaf_in,
    sroot_in,
    smid_in,
    slow_in,
    oroot_in,
    omid_in,
    olow_in,
    gram_out,
    next_out,
    iface_out,
    mroot_out,
    mmid_out,
    mlow_out,
    gt,
    ghi,
    glo,
    raw,
    stiff_ref,
    leaf_ref,
    sroot_ref,
    smid_ref,
    slow_ref,
    oroot_ref,
    omid_ref,
    olow_ref,
    own,
    init,
    iv,
    tt,
    tp,
    rs,
    cs,
    cb,
    ag,
    fb,
    fr,
    yl,
    iy,
    gp,
    grs,
    gc,
    gag,
    iface_ref,
    mroot_ref,
    mmid_ref,
    mlow_ref,
    ms,
    mp,
    mxb,
    mxs,
    mrs,
    mc,
    lsem,
    osem,
    gsend,
    grecv,
    psend,
    precv,
    hsend,
    hrecv,
    xsend,
    xrecv,
    csend,
    crecv,
    ysend,
    yrecv,
    fsend,
    frecv,
):
    leaf = lax.axis_index("leaf")
    mode = lax.axis_index("mode")
    q = leaf // 16
    j = leaf % 16
    base = q * 16
    core = j % 2
    chip = j // 2
    chips = [((chip // 4 + dz) % 2) * 4 + (chip + dx) % 4 for dz, dx in NEAR_FIRST]
    right = (mode + 1) % 4
    left = (mode + 3) % 4
    across = (mode + 2) % 4
    modes = (right, left, across)
    partner = q + 1 - 2 * (q % 2)
    half_base = q - q % 2
    far0 = (q + 2) % 4
    far1 = (partner + 2) % 4
    quarters = (far0, far1, partner)

    loads = [pltpu.make_async_copy(coupling_ref.at[h], raw.at[h], lsem.at[h]) for h in range(3)]
    small = [
        (sroot_in, sroot_ref),
        (smid_in, smid_ref),
        (slow_in, slow_ref),
        (oroot_in, oroot_ref),
        (omid_in, omid_ref),
        (olow_in, olow_ref),
        (stiff_in, stiff_ref),
        (leaf_in, leaf_ref),
    ]
    loads += [pltpu.make_async_copy(a, b, lsem.at[3 + n]) for n, (a, b) in enumerate(small)]
    for load in loads:
        load.start()
    barrier = pltpu.get_barrier_semaphore()

    def greet_group(d, carry):
        pl.semaphore_signal(
            barrier, inc=1, device_id=(base + (j + d) % 16, mode), device_id_type=MESH
        )
        return carry

    for peer in modes:
        pl.semaphore_signal(barrier, inc=1, device_id=(leaf, peer), device_id_type=MESH)
    for peer in quarters:
        for d in range(4):
            pl.semaphore_signal(
                barrier, inc=1, device_id=(peer * 16 + j, (mode + d) % 4), device_id_type=MESH
            )
    lax.fori_loop(1, 16, greet_group, 0)
    for load in loads[3:]:
        load.wait()
    own[0:8] = jnp.concatenate([sroot_ref[...] * SCALE, column(oroot_ref)], axis=1)
    own[8:24] = jnp.concatenate([smid_ref[...] * SCALE, column(omid_ref)], axis=1)
    own[24:56] = jnp.concatenate([slow_ref[...] * SCALE, column(olow_ref)], axis=1)
    init[q] = own[0:24]
    for h in range(3):
        loads[h].wait()
        gt[h, mode] = raw[h].T
    pl.semaphore_wait(barrier, 30)

    def part(c, h, n):
        return gt.at[h, c, pl.ds(64 * n, 64)]

    def chunk(h, kind):
        c, n, peer = (
            (mode, 0, right),
            (mode, 1, left),
            (mode, 1, right),
            (mode, 0, left),
            (left, 0, right),
            (right, 1, left),
        )[kind]
        return remote(part(c, h, n), part(c, h, n), gsend.at[h, kind], grecv.at[h, kind], leaf, peer)

    def chunk_in(h, kind):
        c, n = ((left, 0), (right, 1), (left, 1), (right, 0), (across, 0), (across, 1))[kind]
        return remote(part(c, h, n), part(c, h, n), gsend.at[h, kind], grecv.at[h, kind], leaf, right)

    for kinds in ((0, 1), (2, 3)):
        for h in range(3):
            for kind in kinds:
                chunk(h, kind).start()

    def quarter_copy(src, dst, phase, peer):
        return remote(src, dst, csend.at[phase, peer], crecv.at[phase, q], peer * 16 + j, mode)

    def quarter_in(dst, phase, peer):
        return remote(dst, dst, csend.at[phase, peer], crecv.at[phase, peer], peer * 16 + j, mode)

    top = pl.ds(0, 8)
    init_out = [
        quarter_copy(init.at[q, top], init.at[q, top], 0, far0),
        quarter_copy(init.at[q, top], init.at[q, top], 0, far1),
        quarter_copy(init.at[q], init.at[q], 0, partner),
    ]
    for copy in init_out:
        copy.start()
    quarter_in(init.at[partner], 0, partner).wait_recv()
    quarter_in(init.at[far0, top], 0, far0).wait_recv()
    quarter_in(init.at[far1, top], 0, far1).wait_recv()

    low_lanes = lax.broadcasted_iota(jnp.int32, (16, 128), 1) < 64

    def packs(a, b):
        return (
            jnp.where(low_lanes, a, pltpu.roll(b, 64, 1)),
            jnp.where(low_lanes, pltpu.roll(a, 64, 1), b),
        )

    iroot, wroot = packs(
        jnp.concatenate([init[0, 0:8], init[1, 0:8]], axis=0),
        jnp.concatenate([init[2, 0:8], init[3, 0:8]], axis=0),
    )
    imid, wmid = packs(init[half_base, 8:24], init[half_base + 1, 8:24])
    ilow, wlow = packs(own[24:40], own[40:56])
    state = [iroot, imid, ilow]
    omega = [wroot, wmid, wlow]

    def group_start(phase, src_of, dst):
        def one(d, carry):
            t = (j + d) % 16
            remote(src_of(t), dst, psend.at[phase], precv.at[phase], base + t, mode).start()
            return carry

        lax.fori_loop(1, 16, one, 0)

    def group_all(phase, landing):
        some = landing.at[pl.ds(0, 15)]
        return remote(some, some, psend.at[phase], precv.at[phase], base + (j + 1) % 16, mode)

    def spread_start(s, h):
        ag[s, h, j] = state[h]
        group_start(3 * s + h, lambda t: ag.at[s, h, j], ag.at[s, h, j])

    def spread_wait(s, h):
        group_all(3 * s + h, ag.at[s, h]).wait_recv()
        for n in range(16):
            block = ag[s, h, n]
            turned = pltpu.roll(block, 64, 1)
            if h == 0:
                for k in range(2):
                    iv[root_row(k, n) : root_row(k, n) + 8, :] = block[8 * k : 8 * k + 8]
                    iv[root_row(k + 2, n) : root_row(k + 2, n) + 8, :] = turned[8 * k : 8 * k + 8]
            elif h == 1:
                iv[mid_row(0, n) : mid_row(0, n) + 16, :] = block
                iv[mid_row(1, n) : mid_row(1, n) + 16, :] = turned
            else:
                iv[low_row(n) : low_row(n) + 16, :] = block
                iv[low_row(n) + 16 : low_row(n) + 32, :] = turned

    def pack_terms(s, h):
        for n in range(16):
            if h == 0:
                a, b = [
                    jnp.concatenate(
                        [tt[root_row(k, n) : root_row(k, n) + 8], tt[root_row(k + 1, n) : root_row(k + 1, n) + 8]],
                        axis=0,
                    )
                    for k in (0, 2)
                ]
            elif h == 1:
                a, b = [tt[mid_row(k, n) : mid_row(k, n) + 16] for k in range(2)]
            else:
                a, b = tt[low_row(n) : low_row(n) + 16], tt[low_row(n) + 16 : low_row(n) + 32]
            tp[s, h, n] = jnp.where(low_lanes, a, b)

    def reduce_start(s, h):
        group_start(9 + 3 * s + h, lambda t: tp.at[s, h, t], rs.at[s, h, j])
        rs[s, h, j] = tp[s, h, j]

    def reduce_end(s, h):
        group_all(9 + 3 * s + h, rs.at[s, h]).wait_recv()
        total = rs[s, h, 0]
        for n in range(1, 16):
            total = total + rs[s, h, n]
        return total

    for h in range(3):
        spread_start(0, h)

    coord = lax.broadcasted_iota(jnp.int32, (1, 128), 1)
    live = jnp.concatenate([(coord < sizes_ref[n]).astype(F32) for n in range(4)], axis=1)
    stiff = stiff_ref[...]
    inverse = live / stiff
    weighted = inverse * inverse
    m = leaf_ref[...] * live * SCALE

    def split_chunk(c, h):
        ghi[h, c], glo[h, c] = halves(gt[h, c])

    def apply_chunk(c, h):
        first = pl.multiple_of(h * 512 + c * 128, 128)
        high, low = halves(iv[pl.ds(first, 128), :][:, 0:64].T)
        both = nn16(jnp.concatenate([high, low], axis=0), ghi[h, c])
        return both[0:64] + both[64:128] + nn16(high, glo[h, c])

    def mass_chunk(c, h):
        high, low = halves(gt[h, c] * weighted)
        mine = jnp.concatenate([ghi[h, mode], glo[h, mode]], axis=0)
        both = nt16(high, mine)
        ms[h, pl.ds(pl.multiple_of(c * 128, 128), 128), :] = (
            both[:, 0:128] + both[:, 128:256] + nt16(low, mine[0:128])
        )

    for h in range(3):
        for kind in (0, 1):
            chunk_in(h, kind).wait_recv()
            chunk(h, kind + 4).start()
        split_chunk(mode, h)
    for h in range(3):
        spread_wait(0, h)
    coupled = apply_chunk(mode, 0) + apply_chunk(mode, 1) + apply_chunk(mode, 2)
    for h in range(3):
        chunk_in(h, 2).wait_recv()
        chunk_in(h, 3).wait_recv()
        for c in (left, right):
            split_chunk(c, h)
            coupled = coupled + apply_chunk(c, h)
            mass_chunk(c, h)
        mass_chunk(mode, h)
    for h in range(3):
        chunk_in(h, 4).wait_recv()
        chunk_in(h, 5).wait_recv()
        split_chunk(across, h)
        coupled = coupled + apply_chunk(across, h)

    def to_chip(src, dst, phase, t):
        return remote(src, dst, hsend.at[phase, t], hrecv.at[phase, chip], base + 2 * t + core, mode)

    def from_chip(dst, phase, t):
        return remote(dst, dst, hsend.at[phase, t], hrecv.at[phase, t], base + 2 * t + core, mode)

    mass_core = remote(mp.at[1 - core], mxb, xsend.at[0], xrecv.at[0], leaf + 1 - 2 * core, mode)

    def pack_masses():
        for t in range(16):
            for k in range(4):
                mp[t % 2, t // 2, 8 * k : 8 * k + 8] = ms[0, 128 * k + 8 * t : 128 * k + 8 * t + 8]
            for k in range(2):
                mp[t % 2, t // 2, 32 + 16 * k : 48 + 16 * k] = ms[
                    1, 256 * k + 16 * t : 256 * k + 16 * t + 16
                ]
            mp[t % 2, t // 2, 64:96] = ms[2, 32 * t : 32 * t + 32]

    def y_copy(ref, phase, k):
        return remote(ref.at[mode], ref.at[mode], ysend.at[phase, k], yrecv.at[phase, k], leaf, modes[k])

    def y_in(ref, phase, k):
        came = ref.at[(left, right, across)[k]]
        return remote(came, came, ysend.at[phase, k], yrecv.at[phase, k], leaf, right)

    for s in range(ITERS):
        last = s == ITERS - 1
        if s > 0:
            coupled = jnp.zeros((64, 512), F32)
            for h in (2, 1, 0):
                spread_wait(s, h)
                high, low = halves(iv[512 * h : 512 * h + 512, :][:, 0:64].T)
                both = nn16(jnp.concatenate([high, low], axis=0), ghi[h].reshape(512, 512))
                coupled = coupled + (both[0:64] + both[64:128] + nn16(high, glo[h].reshape(512, 512)))
        modal_mass = live * m - inverse * coupled
        m = inverse * modal_mass
        high, low = halves(m)
        twice = jnp.concatenate([high, high], axis=0)
        four = jnp.concatenate([twice, low, low], axis=0)
        for h in range(3):
            both = nt16(ghi[h].reshape(512, 512), four)
            tt[512 * h : 512 * h + 512, :] = (
                both[:, 0:128] + both[:, 128:256] + nt16(glo[h].reshape(512, 512), twice)
            )
            pack_terms(s, h)
            reduce_start(s, h)
        if last:
            yl[mode] = m
            for k in range(3):
                y_copy(yl, 0, k).start()
        if s == 0:
            for h in range(3):
                mass_chunk(across, h)
            pack_masses()
            mass_core.start()
        if last:
            heavy = m * stiff
            break
        cs[s, 0] = reduce_end(s, 0)
        for peer in (far0, far1, partner):
            quarter_copy(cs.at[s, 0], cb.at[s, 0, q], 1 + s, peer).start()
        cs[s, 1] = reduce_end(s, 1)
        quarter_copy(cs.at[s, 1], cb.at[s, 1, q], 3 + s, partner).start()
        state[2] = (state[2] - reduce_end(s, 2)) / omega[2]
        spread_start(s + 1, 2)
        if s == 0:
            mass_core.wait_recv()
            mxs[...] = mp[core] + mxb[...]
            for t in reversed(chips):
                to_chip(mxs.at[t], mrs.at[chip], 0, t).start()
            mrs[chip] = mxs[chip]
        for peer in (partner, far0, far1):
            quarter_in(cb.at[s, 0, peer], 1 + s, peer).wait_recv()
        gone = (cs[s, 0] + cb[s, 0, partner]) + (cb[s, 0, far0] + cb[s, 0, far1])
        state[0] = (state[0] - gone) / omega[0]
        spread_start(s + 1, 0)
        quarter_in(cb.at[s, 1, partner], 3 + s, partner).wait_recv()
        state[1] = (state[1] - (cs[s, 1] + cb[s, 1, partner])) / omega[1]
        spread_start(s + 1, 1)
        if s == ITERS - 2:
            gp[0:16] = state[0]
            gp[16:32] = pltpu.roll(state[0], 64, 1)
            piece = pl.multiple_of(16 * (q // 2) + 8 * (q % 2), 8)
            iy[mode, 0:8] = gp[pl.ds(piece, 8)]
            odd = (q % 2) == 1
            iy[mode, 8:24] = jnp.where(odd, pltpu.roll(state[1], 64, 1), state[1])
            iy[mode, 24:40] = state[2]
            iy[mode, 40:56] = pltpu.roll(state[2], 64, 1)
            for k in range(3):
                y_copy(iy, 1, k).start()

    total = reduce_end(ITERS - 1, 0)
    turned = pltpu.roll(total, 64, 1)
    for k in range(2):
        fb[k, 0:8] = total[8 * k : 8 * k + 8]
        fb[k + 2, 0:8] = turned[8 * k : 8 * k + 8]

    def owner_copy(peer, d, rows):
        rows = pl.ds(0, rows)
        to = (mode + d) % 4
        return remote(
            fb.at[peer, rows], fr.at[mode, q, rows], fsend.at[peer, to], frecv.at[q, mode], peer * 16 + j, to
        )

    def owner_in(peer, c, rows):
        ref = fr.at[c, peer, pl.ds(0, rows)]
        return remote(ref, ref, fsend.at[peer, c], frecv.at[peer, c], peer * 16 + j, right)

    for peer in (far0, far1):
        for d in (2, 1, 3, 0):
            owner_copy(peer, d, 8).start()
    total = reduce_end(ITERS - 1, 1)
    turned = pltpu.roll(total, 64, 1)
    odd = (q % 2) == 1
    fb[q, 8:24] = jnp.where(odd, turned, total)
    fb[partner, 8:24] = jnp.where(odd, total, turned)
    for d in (2, 1, 3, 0):
        owner_copy(partner, d, 24).start()
    total = reduce_end(ITERS - 1, 2)
    fb[q, 24:40] = total
    fb[q, 40:56] = pltpu.roll(total, 64, 1)
    for d in (2, 1, 3):
        owner_copy(q, d, 56).start()
    fr[mode, q] = fb[q]

    for k in range(3):
        y_in(yl, 0, k).wait_recv()
        y_in(iy, 1, k).wait_recv()
    blocks = [nt(yl[c], heavy) for c in range(4)]
    results = [
        pltpu.make_async_copy(a, b, osem.at[n])
        for n, (a, b) in enumerate(
            (
                (yl, next_out),
                (iface_ref, iface_out),
                (mroot_ref, mroot_out),
                (mmid_ref, mmid_out),
                (mlow_ref, mlow_out),
                (gag, gram_out),
            )
        )
    ]
    results[0].start()
    for peer in (far0, far1):
        for d in range(4):
            owner_in(peer, (mode + d) % 4, 8).wait_recv()
    for d in range(4):
        owner_in(partner, (mode + d) % 4, 24).wait_recv()
    for d in range(1, 4):
        owner_in(q, (mode + d) % 4, 56).wait_recv()
    weights = pltpu.roll(own[...], 64, 1)
    for c in range(4):
        near = fr[c, q, 0:24] + fr[c, partner, 0:24]
        near = jnp.concatenate(
            [near[0:8] + (fr[c, far0, 0:8] + fr[c, far1, 0:8]), near[8:24], fr[c, q, 24:56]], axis=0
        )
        iface_ref[c] = (iy[c] - near) / weights
    results[1].start()
    heavy_own = (iface_ref[mode] * weights)[:, 0:64].T
    blocks = [
        (blocks[c] + nt(iface_ref[c][:, 0:64].T, heavy_own)) * (1.0 / ROWS) for c in range(4)
    ]
    gp[...] = jnp.concatenate(
        [jnp.concatenate(blocks[0:2], axis=0), jnp.concatenate(blocks[2:4], axis=0)], axis=1
    )

    def rows8(t):
        return pl.ds(pl.multiple_of(8 * t, 8), 8)

    group_start(18, lambda t: gp.at[rows8(t)], grs.at[j])
    grs[j] = gp[rows8(j)]
    for t in chips:
        from_chip(mrs.at[t], 0, t).wait_recv()
    total = mrs[0]
    for t in range(1, 8):
        total = total + mrs[t]
    ms[0, 0:96] = total
    mid_of = pl.ds(pl.multiple_of(32 + 16 * (q % 2), 8), 16)
    mid_to = pl.ds(pl.multiple_of(48 - 16 * (q % 2), 8), 16)
    mass_out = [quarter_copy(ms.at[0, rows8(k)], mc.at[q, top], 5, k) for k in quarters]
    mass_out.append(quarter_copy(ms.at[0, mid_to], mc.at[q, pl.ds(8, 16)], 6, partner))
    for copy in mass_out:
        copy.start()

    group_all(18, grs).wait_recv()
    total = grs[0]
    for t in range(1, 16):
        total = total + grs[t]
    gc[mode, q] = total

    def gram_copy(peer, d):
        to = (mode + d) % 4
        ref = gc.at[mode, q]
        return remote(ref, ref, fsend.at[peer + 4, to], frecv.at[q + 4, mode], peer * 16 + j, to)

    def gram_in(peer, c):
        ref = gc.at[c, peer]
        return remote(ref, ref, fsend.at[peer + 4, c], frecv.at[peer + 4, c], peer * 16 + j, right)

    for peer in quarters:
        for d in (2, 1, 3, 0):
            gram_copy(peer, d).start()
    for d in (2, 1, 3):
        gram_copy(q, d).start()

    for peer in quarters:
        quarter_in(mc.at[peer, top], 5, peer).wait_recv()
    quarter_in(mc.at[partner, pl.ds(8, 16)], 6, partner).wait_recv()

    def unit(first, count):
        rows = lax.broadcasted_iota(jnp.int32, (count, 128), 0) + first
        cols = lax.broadcasted_iota(jnp.int32, (count, 128), 1) + mode * 128
        return (rows % 512 == cols).astype(F32)

    mroot_ref[...] = (
        ms[0, rows8(q)] + (mc[partner, 0:8] + mc[far0, 0:8] + mc[far1, 0:8]) + unit(leaf * 8, 8)
    )
    mmid_ref[...] = ms[0, mid_of] + mc[partner, 8:24] + unit(leaf * 16, 16)
    mlow_ref[...] = ms[0, 64:96] + unit(leaf * 32, 32)
    for result in results[2:5]:
        result.start()
    for h in range(3):
        for kind in range(6):
            chunk(h, kind).wait_send()
    for copy in init_out:
        copy.wait_send()
    for s in range(ITERS):
        for h in range(3):
            group_all(3 * s + h, ag.at[s, h]).wait_send()
            group_all(9 + 3 * s + h, rs.at[s, h]).wait_send()
    for s in range(ITERS - 1):
        for peer in quarters:
            quarter_copy(cs.at[s, 0], cb.at[s, 0, q], 1 + s, peer).wait_send()
        quarter_copy(cs.at[s, 1], cb.at[s, 1, q], 3 + s, partner).wait_send()
    mass_core.wait_send()
    for t in chips:
        to_chip(mxs.at[t], mrs.at[chip], 0, t).wait_send()
    for k in range(3):
        y_copy(yl, 0, k).wait_send()
        y_copy(iy, 1, k).wait_send()

    for peer in quarters:
        for d in range(4):
            gram_in(peer, (mode + d) % 4).wait_recv()
    for d in range(1, 4):
        gram_in(q, (mode + d) % 4).wait_recv()
    for c in range(4):
        gag[j, c] = (gc[c, 0] + gc[c, 1]) + (gc[c, 2] + gc[c, 3])
    group_start(19, lambda t: gag.at[j], gag.at[j])
    for d in range(4):
        for peer in (far0, far1):
            owner_copy(peer, d, 8).wait_send()
        owner_copy(partner, d, 24).wait_send()
        if d > 0:
            owner_copy(q, d, 56).wait_send()
            gram_copy(q, d).wait_send()
        for peer in quarters:
            gram_copy(peer, d).wait_send()
    for copy in mass_out:
        copy.wait_send()
    group_all(18, grs).wait_send()
    group_all(19, gag).wait_recv()
    results[5].start()
    group_all(19, gag).wait_send()
    for result in results:
        result.wait()


def run_sweeps(leaf_sizes, stiff, coupling, start_leaf, starts, omegas):
    scratch = [
        (3, 4, 128, 512),
        (3, 4, 128, 512),
        (3, 4, 128, 512),
        (3, 512, 128),
        (1, 512),
        (64, 512),
        (8, 64),
        (16, 64),
        (32, 64),
        (1, 8),
        (1, 16),
        (1, 32),
        (56, 128),
        (4, 24, 128),
        (1536, 128),
        (1536, 128),
        (3, 3, 16, 16, 128),
        (3, 3, 16, 16, 128),
        (2, 2, 16, 128),
        (2, 2, 4, 16, 128),
        (3, 3, 16, 16, 128),
        (4, 56, 128),
        (4, 4, 56, 128),
        (4, 64, 512),
        (4, 56, 128),
        (128, 128),
        (16, 8, 128),
        (4, 4, 8, 128),
        (16, 4, 8, 128),
        (4, 56, 128),
        (8, 128),
        (16, 128),
        (32, 128),
        (3, 512, 128),
        (2, 8, 96, 128),
        (8, 96, 128),
        (8, 96, 128),
        (8, 96, 128),
        (4, 24, 128),
    ]
    sems = [(11,), (6,), (3, 6), (3, 6), (20,), (20,), (1, 8), (1, 8), (1,), (1,)]
    sems += [(7, 4), (7, 4), (2, 3), (2, 3), (8, 4), (8, 4)]
    shapes = [(16, 4, 8, 128), (4, 64, 512), (4, 56, 128), (8, 128), (16, 128), (32, 128)]
    return pl.pallas_call(
        sweeps_kernel,
        out_shape=[jax.ShapeDtypeStruct(shape, F32) for shape in shapes],
        in_specs=[pl.BlockSpec(memory_space=pltpu.SMEM)]
        + [pl.BlockSpec(memory_space=pltpu.HBM)] * 9,
        out_specs=[pl.BlockSpec(memory_space=pltpu.HBM)] * 6,
        scratch_shapes=[
            pltpu.VMEM(shape, BF16 if n in (1, 2) else F32) for n, shape in enumerate(scratch)
        ]
        + [pltpu.SemaphoreType.DMA(shape) for shape in sems],
        compiler_params=pltpu.CompilerParams(
            collective_id=0, has_side_effects=True, vmem_limit_bytes=64 * 1024 * 1024
        ),
        name="sweeps",
    )(leaf_sizes, stiff, coupling, start_leaf, *starts, *omegas)


def factor_block(a):
    rows = [a[8 * r : 8 * r + 8, :] for r in range(8)]
    sub = lax.broadcasted_iota(jnp.int32, (8, 128), 0)
    pivots = []
    for p in range(8):
        cols = []
        for k in range(8):
            lane = 8 * p + k
            cols.append(
                [jnp.broadcast_to(rows[r][:, lane : lane + 1], (8, 128)) for r in range(p, 8)]
            )
        diag = []
        for k in range(8):
            pivot = jnp.broadcast_to(cols[k][0][k : k + 1, :], (8, 128))
            diag.append(pivot)
            scale = 1.0 / pivot
            factors = [c * scale for c in cols[k]]
            factors[0] = jnp.where(sub > k, factors[0], 0.0)
            for k2 in range(k + 1, 8):
                across = jnp.broadcast_to(cols[k2][0][k : k + 1, :], (8, 128))
                cols[k2] = [c - f * across for c, f in zip(cols[k2], factors)]
            lead = jnp.broadcast_to(rows[p][k : k + 1, :], (8, 128))
            for r in range(p, 8):
                rows[r] = rows[r] - factors[r - p] * lead
        scale = diag[0]
        for k in range(1, 8):
            scale = jnp.where(sub == k, diag[k], scale)
        pivots.append(lax.rsqrt(scale))
    return jnp.concatenate([row * pivot for row, pivot in zip(rows, pivots)], axis=0)


def finish_kernel(
    gram_in,
    next_in,
    iface_in,
    mroot_in,
    mmid_in,
    mlow_in,
    leaf_out,
    root_out,
    mid_out,
    low_out,
    mroot_out,
    mmid_out,
    mlow_out,
    gram_ref,
    next_ref,
    iface_ref,
    full,
    lower,
    sem,
):
    mode = lax.axis_index("mode")
    moves = (
        (gram_in, gram_ref),
        (next_in, next_ref),
        (iface_in, iface_ref),
        (mroot_in, mroot_out),
        (mmid_in, mmid_out),
        (mlow_in, mlow_out),
    )
    moves = [pltpu.make_async_copy(a, b, sem.at[n]) for n, (a, b) in enumerate(moves)]
    for move in moves:
        move.start()
    moves[0].wait()
    low_lanes = lax.broadcasted_iota(jnp.int32, (128, 128), 1) < 64
    parts = [jnp.concatenate([gram_ref[t, c] for t in range(16)], axis=0) for c in range(4)]
    turned = [pltpu.roll(part, 64, 1) for part in parts]
    gram = jnp.concatenate(
        [
            jnp.concatenate([jnp.where(low_lanes, parts[c], turned[c + 1]) for c in (0, 2)], axis=1),
            jnp.concatenate([jnp.where(low_lanes, turned[c], parts[c + 1]) for c in (0, 2)], axis=1),
        ],
        axis=0,
    )
    full[:, 0:256] = 0.5 * (gram + gram.T)
    r = lax.broadcasted_iota(jnp.int32, (256, 256), 0)
    c = lax.broadcasted_iota(jnp.int32, (256, 256), 1)
    full[:, 256:512] = (r == c).astype(F32)
    unit = (
        lax.broadcasted_iota(jnp.int32, (64, 64), 0) == lax.broadcasted_iota(jnp.int32, (64, 64), 1)
    ).astype(F32)
    for k in range(4):
        first = 64 * k
        block = full[first : first + 64, first : first + 64]
        weight = factor_block(jnp.concatenate([block, unit], axis=1))[:, 64:128]
        right = 128 * (k // 2)
        panel = nn(weight, full[first : first + 64, right:512])
        lower[first : first + 64, :] = panel[:, 256 - right : 512 - right]
        if k < 3:
            below = panel[:, first + 64 - right : 256 - right]
            full[first + 64 : 256, right:512] = full[first + 64 : 256, right:512] - tn(below, panel)
    own = lower[pl.ds(pl.multiple_of(mode * 64, 64), 64), :]
    for move in moves[1:]:
        move.wait()
    leaf_out[...] = nn(own, next_ref[...].reshape(256, 512))
    iface = jnp.concatenate([iface_ref[c][:, 0:64] for c in range(4)], axis=1)
    done = nt(iface, own)
    root_out[...] = done[0:8]
    mid_out[...] = done[8:24]
    low_out[...] = done[24:56]


def run_finish(gram, modal, iface, masses):
    vmem = pl.BlockSpec(memory_space=pltpu.VMEM)
    hbm = pl.BlockSpec(memory_space=pltpu.HBM)
    shapes = [(64, 512), (8, 64), (16, 64), (32, 64), (8, 128), (16, 128), (32, 128)]
    return pl.pallas_call(
        finish_kernel,
        out_shape=[jax.ShapeDtypeStruct(shape, F32) for shape in shapes],
        in_specs=[hbm] * 6,
        out_specs=[vmem] * 4 + [hbm] * 3,
        scratch_shapes=[
            pltpu.VMEM((16, 4, 8, 128), F32),
            pltpu.VMEM((4, 64, 512), F32),
            pltpu.VMEM((4, 56, 128), F32),
            pltpu.VMEM((256, 512), F32),
            pltpu.VMEM((256, 256), F32),
            pltpu.SemaphoreType.DMA((6,)),
        ],
        compiler_params=pltpu.CompilerParams(vmem_limit_bytes=64 * 1024 * 1024),
        name="finish",
    )(gram, modal, iface, *masses)


def local(
    leaf_sizes,
    leaf_stiffness,
    coupling,
    omega_root,
    omega_mid,
    omega_low,
    start_leaf,
    start_root,
    start_mid,
    start_low,
):
    gram, modal, iface, *masses = run_sweeps(
        leaf_sizes,
        leaf_stiffness.reshape(1, -1),
        coupling,
        start_leaf,
        [start_root.T, start_mid.T, start_low.T],
        [omega_root.reshape(1, -1), omega_mid.reshape(1, -1), omega_low.reshape(1, -1)],
    )
    leaf, root, mid, low, *masses = run_finish(gram, modal, iface, masses)
    return (leaf, root.T, mid.T, low.T, *masses)


def solution(mesh):
    placed = (
        P("leaf"),
        P("leaf"),
        P(None, "leaf", "mode"),
        P("leaf"),
        P("leaf"),
        P("leaf"),
        P("mode", "leaf"),
        P("mode", "leaf"),
        P("mode", "leaf"),
        P("mode", "leaf"),
    )
    return jax.shard_map(
        local,
        mesh=mesh,
        in_specs=placed,
        out_specs=(
            P("mode", "leaf"),
            P("mode", "leaf"),
            P("mode", "leaf"),
            P("mode", "leaf"),
            P("leaf", "mode"),
            P("leaf", "mode"),
            P("leaf", "mode"),
        ),
        check_vma=False,
    )
```

time: 1620 us -> 118 us (0.07)
  waiting for transfers between devices: 1060 us -> 0 us
  blocking collectives: 223 us -> 0 us
  other arithmetic: 196 us -> 0 us
  Pallas kernels: 0 us -> 117 us
  local copies, waits for them, and re-layouts: 64 us -> 0 us
  matrix products: 49.6 us -> 0 us
  between operations: 19.8 us -> 0.8 us
    psum x3 -> x0, waiting for transfers between devices: 529 us -> none  [local(): gram_leaf = lax.psum(gram_part, 'leaf')]
    unnamed x10 -> x0, waiting for transfers between devices: 527 us -> none
    all_gather x9 -> x0, blocking collectives: 223 us -> none  [the longest x3 160 us: local(): lax.all_gather(interface_own, 'leaf', axis=1, tiled=True)]
    another operation x30 -> x0, other arithmetic: 170 us -> none  [the longest x20 105 us: local(): lower_factor = jnp.linalg.cholesky(gram_matrix)]
    pallas_call x0 -> x2, Pallas kernels: none -> 117 us  [the longest x1 105 us: run_sweeps(): pl.pallas_call(sweeps_kernel, out_shape=[jax.ShapeDtypeStruct(shape, F32)...]
    dot_general x10 -> x0, matrix products: 32.1 us -> none  [the longest x3 14.7 us: local(): jnp.einsum('hpi,hli->pl', stacked, full_coupling, precision=precise)]
    another operation x36 -> x0, local copies, waits for them, and re-layouts: 22.8 us -> none  [the longest x24 17.7 us: local(): jax.scipy.linalg.solve_triangular(lower_factor, next_full, lower=True)]
    another operation x15 -> x0, matrix products: 17.6 us -> none  [the longest x9 12.8 us: local(): jax.scipy.linalg.solve_triangular(lower_factor, next_full, lower=True)]
  transfers between devices with their start and end apart: 7 -> 0, of which waited for: 6 -> 0; matrix products, arithmetic and copies ran while one was open for 1% -> 0% of each run, Pallas kernels for 0% -> 0%
where the time goes in v1:
time: 118 us
  Pallas kernels  117 us (99%)
    pallas_call x1, Pallas kernels, run_sweeps(): pl.pallas_call(sweeps_kernel, out_shape=[jax.ShapeDtypeStruct(shape, F32)...  105 us
    pallas_call x1, Pallas kernels, run_finish(): pl.pallas_call(finish_kernel, out_shape=[jax.ShapeDtypeStruct(shape, F32)...  12 us

profile of v1, /device:TPU:1, one launch (start us, length us, event | category | flops | bytes accessed | tf_op | source)
XLA Modules:
  0.0 118.0 jit_solution(5720053969329514094)
XLA Ops:
  0.6 105.2 %sweeps.1 = (f32[16,4,8,128]{3,2,1,0:T(8,128)}, f32[4,64,512]{2,1,0:T(8,128)}, f32[4,56,128]{2,1,0:T(8,128)}, f32[8,128]{1,0:T(8,128)}, f32[16,128]{1,0:T(8,128)}, /*index=5*/f32[32,128]{1,0:T(8,128)}) custom-call(s32[4]{0:T(128)} %sizes_ref.1, f32[1,512]{1,0:T(1,128)} %bitcast.13, f32[3,512,128]{2,1,0:T(8,128)} %coupling_ref.1, f32[64,512]{1,0:T(8,128)} %leaf_in.1, ...), custom_call_target="tpu_custom_call" | custom-call | tf_op jit(solution)/shard_map/sweeps/pallas_call | solution.py:686
  105.9 12.0 %finish.1 = (f32[64,512]{1,0:T(8,128)}, f32[8,64]{1,0:T(8,128)}, f32[16,64]{1,0:T(8,128)}, f32[32,64]{1,0:T(8,128)}, f32[8,128]{1,0:T(8,128)}, /*index=5*/f32[16,128]{1,0:T(8,128)}, f32[32,128]{1,0:T(8,128)}) custom-call(f32[16,4,8,128]{3,2,1,0:T(8,128)} %get-tuple-element.20.gram_in, f32[4,64,512]{2,1,0:T(8,128)} %get-tuple-element.21.next_in, ...), custom_call_target="tpu_custom_call" | custom-call | tf_op jit(solution)/shard_map/finish/pallas_call | solution.py:810

commit v2 on v1

--- a/solution.py
+++ b/solution.py
@@ -106,6 +106,8 @@
     iv,
     tt,
     tp,
+    xb,
+    xs,
     rs,
     cs,
     cb,
@@ -274,12 +276,42 @@
         some = landing.at[pl.ds(0, 15)]
         return remote(some, some, psend.at[phase], precv.at[phase], base + (j + 1) % 16, mode)
 
+    mine = 8 * core + chip
+    other = leaf + 1 - 2 * core
+
+    def chips_start(phase, src_of, dst):
+        for t in reversed(chips):
+            remote(src_of(t), dst, psend.at[phase], precv.at[phase], base + 2 * t + core, mode).start()
+
+    def chips_all(phase, landing):
+        some = landing.at[pl.ds(0, 7)]
+        return remote(some, some, psend.at[phase], precv.at[phase], other, mode)
+
+    def core_copy(n, src, dst):
+        return remote(src, dst, xsend.at[n], xrecv.at[n], other, mode)
+
     def spread_start(s, h):
-        ag[s, h, j] = state[h]
-        group_start(3 * s + h, lambda t: ag.at[s, h, j], ag.at[s, h, j])
+        slot = mine if h == 2 else j
+        ag[s, h, slot] = state[h]
+        block = ag.at[s, h, slot]
+        if h == 2:
+            chips_start(3 * s + h, lambda t: block, block)
+        else:
+            group_start(3 * s + h, lambda t: block, block)
+
+    def pass_on(s, c):
+        blocks = ag.at[s, 2, pl.ds(8 * c, 8)]
+        return core_copy(s, blocks, blocks)
+
+    def spread_forward(s):
+        chips_all(3 * s + 2, ag.at[s, 2]).wait_recv()
+        pass_on(s, core).start()
 
     def spread_wait(s, h):
-        group_all(3 * s + h, ag.at[s, h]).wait_recv()
+        if h == 2:
+            pass_on(s, 1 - core).wait_recv()
+        else:
+            group_all(3 * s + h, ag.at[s, h]).wait_recv()
         for n in range(16):
             block = ag[s, h, n]
             turned = pltpu.roll(block, 64, 1)
@@ -291,8 +323,9 @@
                 iv[mid_row(0, n) : mid_row(0, n) + 16, :] = block
                 iv[mid_row(1, n) : mid_row(1, n) + 16, :] = turned
             else:
-                iv[low_row(n) : low_row(n) + 16, :] = block
-                iv[low_row(n) + 16 : low_row(n) + 32, :] = turned
+                first = low_row(2 * (n % 8) + n // 8)
+                iv[first : first + 16, :] = block
+                iv[first + 16 : first + 32, :] = turned
 
     def pack_terms(s, h):
         for n in range(16):
@@ -308,16 +341,31 @@
                 a, b = [tt[mid_row(k, n) : mid_row(k, n) + 16] for k in range(2)]
             else:
                 a, b = tt[low_row(n) : low_row(n) + 16], tt[low_row(n) + 16 : low_row(n) + 32]
-            tp[s, h, n] = jnp.where(low_lanes, a, b)
+            tp[s, h, n if h == 0 else 8 * (n % 2) + n // 2] = jnp.where(low_lanes, a, b)
+
+    def cross(s, h):
+        return core_copy(1 + 2 * s + h + 1, tp.at[s, h, pl.ds(8 * (1 - core), 8)], xb.at[s, h - 1])
 
     def reduce_start(s, h):
-        group_start(9 + 3 * s + h, lambda t: tp.at[s, h, t], rs.at[s, h, j])
-        rs[s, h, j] = tp[s, h, j]
+        if h > 0:
+            cross(s, h).start()
+            return
+        group_start(9 + 3 * s, lambda t: tp.at[s, 0, t], rs.at[s, 0, j])
+        rs[s, 0, j] = tp[s, 0, j]
+
+    def reduce_middle(s, h):
+        cross(s, h).wait_recv()
+        xs[s, h - 1] = tp[s, h, pl.ds(8 * core, 8)] + xb[s, h - 1]
+        chips_start(9 + 3 * s + h, lambda t: xs.at[s, h - 1, t], rs.at[s, h, chip])
+        rs[s, h, chip] = xs[s, h - 1, chip]
 
     def reduce_end(s, h):
-        group_all(9 + 3 * s + h, rs.at[s, h]).wait_recv()
+        if h == 0:
+            group_all(9 + 3 * s, rs.at[s, h]).wait_recv()
+        else:
+            chips_all(9 + 3 * s + h, rs.at[s, h]).wait_recv()
         total = rs[s, h, 0]
-        for n in range(1, 16):
+        for n in range(1, 16 if h == 0 else 8):
             total = total + rs[s, h, n]
         return total
 
@@ -340,20 +388,19 @@
         both = nn16(jnp.concatenate([high, low], axis=0), ghi[h, c])
         return both[0:64] + both[64:128] + nn16(high, glo[h, c])
 
-    def mass_chunk(c, h):
-        high, low = halves(gt[h, c] * weighted)
+    def project(h):
+        high, low = halves(gt[h].reshape(512, 512) * weighted)
         mine = jnp.concatenate([ghi[h, mode], glo[h, mode]], axis=0)
         both = nt16(high, mine)
-        ms[h, pl.ds(pl.multiple_of(c * 128, 128), 128), :] = (
-            both[:, 0:128] + both[:, 128:256] + nt16(low, mine[0:128])
-        )
+        ms[h] = both[:, 0:128] + both[:, 128:256] + nt16(low, mine[0:128])
 
     for h in range(3):
         for kind in (0, 1):
             chunk_in(h, kind).wait_recv()
             chunk(h, kind + 4).start()
         split_chunk(mode, h)
-    for h in range(3):
+    spread_forward(0)
+    for h in (0, 1, 2):
         spread_wait(0, h)
     coupled = apply_chunk(mode, 0) + apply_chunk(mode, 1) + apply_chunk(mode, 2)
     for h in range(3):
@@ -362,21 +409,27 @@
         for c in (left, right):
             split_chunk(c, h)
             coupled = coupled + apply_chunk(c, h)
-            mass_chunk(c, h)
-        mass_chunk(mode, h)
     for h in range(3):
         chunk_in(h, 4).wait_recv()
         chunk_in(h, 5).wait_recv()
         split_chunk(across, h)
         coupled = coupled + apply_chunk(across, h)
 
-    def to_chip(src, dst, phase, t):
-        return remote(src, dst, hsend.at[phase, t], hrecv.at[phase, chip], base + 2 * t + core, mode)
-
-    def from_chip(dst, phase, t):
-        return remote(dst, dst, hsend.at[phase, t], hrecv.at[phase, t], base + 2 * t + core, mode)
-
-    mass_core = remote(mp.at[1 - core], mxb, xsend.at[0], xrecv.at[0], leaf + 1 - 2 * core, mode)
+    def mass_copy(h, t):
+        rows = pl.ds(32 * h, 32)
+        return remote(
+            mxs.at[t, rows], mrs.at[chip, rows], hsend.at[h, t], hrecv.at[h, chip], base + 2 * t + core, mode
+        )
+
+    def mass_in(h, t):
+        came = mrs.at[t, pl.ds(32 * h, 32)]
+        return remote(came, came, hsend.at[h, t], hrecv.at[h, t], base + 2 * t + core, mode)
+
+    def mass_part(h):
+        for t in reversed(chips):
+            mass_copy(h, t).start()
+
+    mass_core = core_copy(9, mp.at[1 - core], mxb)
 
     def pack_masses():
         for t in range(16):
@@ -399,7 +452,7 @@
         last = s == ITERS - 1
         if s > 0:
             coupled = jnp.zeros((64, 512), F32)
-            for h in (2, 1, 0):
+            for h in (2, 0, 1):
                 spread_wait(s, h)
                 high, low = halves(iv[512 * h : 512 * h + 512, :][:, 0:64].T)
                 both = nn16(jnp.concatenate([high, low], axis=0), ghi[h].reshape(512, 512))
@@ -416,13 +469,15 @@
             )
             pack_terms(s, h)
             reduce_start(s, h)
+        for h in (1, 2):
+            reduce_middle(s, h)
         if last:
             yl[mode] = m
             for k in range(3):
                 y_copy(yl, 0, k).start()
         if s == 0:
             for h in range(3):
-                mass_chunk(across, h)
+                project(h)
             pack_masses()
             mass_core.start()
         if last:
@@ -438,9 +493,8 @@
         if s == 0:
             mass_core.wait_recv()
             mxs[...] = mp[core] + mxb[...]
-            for t in reversed(chips):
-                to_chip(mxs.at[t], mrs.at[chip], 0, t).start()
             mrs[chip] = mxs[chip]
+        mass_part(s)
         for peer in (partner, far0, far1):
             quarter_in(cb.at[s, 0, peer], 1 + s, peer).wait_recv()
         gone = (cs[s, 0] + cb[s, 0, partner]) + (cb[s, 0, far0] + cb[s, 0, far1])
@@ -449,6 +503,7 @@
         quarter_in(cb.at[s, 1, partner], 3 + s, partner).wait_recv()
         state[1] = (state[1] - (cs[s, 1] + cb[s, 1, partner])) / omega[1]
         spread_start(s + 1, 1)
+        spread_forward(s + 1)
         if s == ITERS - 2:
             gp[0:16] = state[0]
             gp[16:32] = pltpu.roll(state[0], 64, 1)
@@ -495,6 +550,7 @@
         owner_copy(q, d, 56).start()
     fr[mode, q] = fb[q]
 
+    mass_part(2)
     for k in range(3):
         y_in(yl, 0, k).wait_recv()
         y_in(iy, 1, k).wait_recv()
@@ -541,8 +597,9 @@
 
     group_start(18, lambda t: gp.at[rows8(t)], grs.at[j])
     grs[j] = gp[rows8(j)]
-    for t in chips:
-        from_chip(mrs.at[t], 0, t).wait_recv()
+    for h in range(3):
+        for t in chips:
+            mass_in(h, t).wait_recv()
     total = mrs[0]
     for t in range(1, 8):
         total = total + mrs[t]
@@ -598,15 +655,22 @@
         copy.wait_send()
     for s in range(ITERS):
         for h in range(3):
-            group_all(3 * s + h, ag.at[s, h]).wait_send()
-            group_all(9 + 3 * s + h, rs.at[s, h]).wait_send()
+            if h == 0:
+                group_all(3 * s, ag.at[s, h]).wait_send()
+                group_all(9 + 3 * s, rs.at[s, h]).wait_send()
+                pass_on(s, core).wait_send()
+                continue
+            (group_all if h == 1 else chips_all)(3 * s + h, ag.at[s, h]).wait_send()
+            chips_all(9 + 3 * s + h, rs.at[s, h]).wait_send()
+            cross(s, h).wait_send()
     for s in range(ITERS - 1):
         for peer in quarters:
             quarter_copy(cs.at[s, 0], cb.at[s, 0, q], 1 + s, peer).wait_send()
         quarter_copy(cs.at[s, 1], cb.at[s, 1, q], 3 + s, partner).wait_send()
     mass_core.wait_send()
-    for t in chips:
-        to_chip(mxs.at[t], mrs.at[chip], 0, t).wait_send()
+    for h in range(3):
+        for t in chips:
+            mass_copy(h, t).wait_send()
     for k in range(3):
         y_copy(yl, 0, k).wait_send()
         y_copy(iy, 1, k).wait_send()
@@ -657,6 +721,8 @@
         (1536, 128),
         (1536, 128),
         (3, 3, 16, 16, 128),
+        (3, 2, 8, 16, 128),
+        (3, 2, 8, 16, 128),
         (3, 3, 16, 16, 128),
         (2, 2, 16, 128),
         (2, 2, 4, 16, 128),
@@ -680,7 +746,7 @@
         (8, 96, 128),
         (4, 24, 128),
     ]
-    sems = [(11,), (6,), (3, 6), (3, 6), (20,), (20,), (1, 8), (1, 8), (1,), (1,)]
+    sems = [(11,), (6,), (3, 6), (3, 6), (20,), (20,), (3, 8), (3, 8), (10,), (10,)]
     sems += [(7, 4), (7, 4), (2, 3), (2, 3), (8, 4), (8, 4)]
     shapes = [(16, 4, 8, 128), (4, 64, 512), (4, 56, 128), (8, 128), (16, 128), (32, 128)]
     return pl.pallas_call(
@@ -707,23 +773,29 @@
     for p in range(8):
         cols = []
         for k in range(8):
-            lane = 8 * p + k
-            cols.append(
-                [jnp.broadcast_to(rows[r][:, lane : lane + 1], (8, 128)) for r in range(p, 8)]
-            )
+            pick = jnp.full((8, 128), 8 * p + k, jnp.int32)
+            cols.append([jnp.take_along_axis(rows[r], pick, axis=1) for r in range(p, 8)])
         diag = []
-        for k in range(8):
-            pivot = jnp.broadcast_to(cols[k][0][k : k + 1, :], (8, 128))
-            diag.append(pivot)
-            scale = 1.0 / pivot
-            factors = [c * scale for c in cols[k]]
-            factors[0] = jnp.where(sub > k, factors[0], 0.0)
-            for k2 in range(k + 1, 8):
-                across = jnp.broadcast_to(cols[k2][0][k : k + 1, :], (8, 128))
-                cols[k2] = [c - f * across for c, f in zip(cols[k2], factors)]
-            lead = jnp.broadcast_to(rows[p][k : k + 1, :], (8, 128))
+        for k in range(0, 8, 2):
+            head, cross = [jnp.broadcast_to(cols[k][0][n : n + 1, :], (8, 128)) for n in (k, k + 1)]
+            tail = jnp.broadcast_to(cols[k + 1][0][k + 1 : k + 2, :], (8, 128))
+            det = head * tail - cross * cross
+            inv0 = 1.0 / head
+            inv1 = head * (1.0 / det)
+            ratio = cross * inv0
+            diag += [head, det * inv0]
+            first = [c * inv0 for c in cols[k]]
+            first[0] = jnp.where(sub > k, first[0], 0.0)
+            second = [(c - f * cross) * inv1 for c, f in zip(cols[k + 1], first)]
+            second[0] = jnp.where(sub > k + 1, second[0], 0.0)
+            for k2 in range(k + 2, 8):
+                up0 = jnp.broadcast_to(cols[k2][0][k : k + 1, :], (8, 128))
+                up1 = jnp.broadcast_to(cols[k2][0][k + 1 : k + 2, :], (8, 128)) - ratio * up0
+                cols[k2] = [c - (f * up0 + g * up1) for c, f, g in zip(cols[k2], first, second)]
+            lead0 = jnp.broadcast_to(rows[p][k : k + 1, :], (8, 128))
+            lead1 = jnp.broadcast_to(rows[p][k + 1 : k + 2, :], (8, 128)) - ratio * lead0
             for r in range(p, 8):
-                rows[r] = rows[r] - factors[r - p] * lead
+                rows[r] = rows[r] - (first[r - p] * lead0 + second[r - p] * lead1)
         scale = diag[0]
         for k in range(1, 8):
             scale = jnp.where(sub == k, diag[k], scale)
@@ -775,10 +847,14 @@
         ],
         axis=0,
     )
-    full[:, 0:256] = 0.5 * (gram + gram.T)
+    gram = 0.5 * (gram + gram.T)
     r = lax.broadcasted_iota(jnp.int32, (256, 256), 0)
     c = lax.broadcasted_iota(jnp.int32, (256, 256), 1)
-    full[:, 256:512] = (r == c).astype(F32)
+    corner = jnp.where(r == c, gram, 0.0)
+    down = lax.rsqrt(jnp.sum(corner, axis=1, keepdims=True))
+    over = lax.rsqrt(jnp.sum(corner, axis=0, keepdims=True))
+    full[:, 0:256] = gram * down * over
+    full[:, 256:512] = jnp.where(r == c, jnp.broadcast_to(down, (256, 256)), 0.0)
     unit = (
         lax.broadcasted_iota(jnp.int32, (64, 64), 0) == lax.broadcasted_iota(jnp.int32, (64, 64), 1)
     ).astype(F32)

time: 118 us -> 112 us (0.949)
  Pallas kernels: 117 us -> 111 us
    pallas_call x1, Pallas kernels: 105 us -> 101 us  [run_sweeps(): pl.pallas_call(sweeps_kernel, out_shape=[jax.ShapeDtypeStruct(shape, F32)...]
    pallas_call x1, Pallas kernels: 12 us -> 9.89 us  [run_finish(): pl.pallas_call(finish_kernel, out_shape=[jax.ShapeDtypeStruct(shape, F32)...]
where the time goes in v2:
time: 112 us
  Pallas kernels  111 us (99%)
    pallas_call x1, Pallas kernels, run_sweeps(): pl.pallas_call(sweeps_kernel, out_shape=[jax.ShapeDtypeStruct(shape, F32)...  101 us
    pallas_call x1, Pallas kernels, run_finish(): pl.pallas_call(finish_kernel, out_shape=[jax.ShapeDtypeStruct(shape, F32)...  9.89 us

profile of v2, /device:TPU:1, one launch (start us, length us, event | category | flops | bytes accessed | tf_op | source)
XLA Modules:
  0.0 112.0 jit_solution(2484348721757851708)
XLA Ops:
  0.6 101.3 %sweeps.1 = (f32[16,4,8,128]{3,2,1,0:T(8,128)}, f32[4,64,512]{2,1,0:T(8,128)}, f32[4,56,128]{2,1,0:T(8,128)}, f32[8,128]{1,0:T(8,128)}, f32[16,128]{1,0:T(8,128)}, /*index=5*/f32[32,128]{1,0:T(8,128)}) custom-call(s32[4]{0:T(128)} %sizes_ref.1, f32[1,512]{1,0:T(1,128)} %bitcast.13, f32[3,512,128]{2,1,0:T(8,128)} %coupling_ref.1, f32[64,512]{1,0:T(8,128)} %leaf_in.1, ...), custom_call_target="tpu_custom_call" | custom-call | tf_op jit(solution)/shard_map/sweeps/pallas_call | solution.py:752
  102.0 9.9 %finish.1 = (f32[64,512]{1,0:T(8,128)}, f32[8,64]{1,0:T(8,128)}, f32[16,64]{1,0:T(8,128)}, f32[32,64]{1,0:T(8,128)}, f32[8,128]{1,0:T(8,128)}, /*index=5*/f32[16,128]{1,0:T(8,128)}, f32[32,128]{1,0:T(8,128)}) custom-call(f32[16,4,8,128]{3,2,1,0:T(8,128)} %get-tuple-element.20.gram_in, f32[4,64,512]{2,1,0:T(8,128)} %get-tuple-element.21.next_in, ...), custom_call_target="tpu_custom_call" | custom-call | tf_op jit(solution)/shard_map/finish/pallas_call | solution.py:886

commit v3 on v2

--- a/solution.py
+++ b/solution.py
@@ -165,6 +165,20 @@
     far1 = (partner + 2) % 4
     quarters = (far0, far1, partner)
 
+    around = [(j + d) % 16 for d in range(1, 16)]
+    barrier = pltpu.get_barrier_semaphore()
+
+    def greet(to_leaf, to_mode):
+        pl.semaphore_signal(barrier, inc=1, device_id=(to_leaf, to_mode), device_id_type=MESH)
+
+    for peer in quarters:
+        for to in (mode,) + modes:
+            greet(peer * 16 + j, to)
+    for to in modes:
+        greet(leaf, to)
+    for t in around:
+        greet(base + t, mode)
+
     loads = [pltpu.make_async_copy(coupling_ref.at[h], raw.at[h], lsem.at[h]) for h in range(3)]
     small = [
         (sroot_in, sroot_ref),
@@ -179,22 +193,6 @@
     loads += [pltpu.make_async_copy(a, b, lsem.at[3 + n]) for n, (a, b) in enumerate(small)]
     for load in loads:
         load.start()
-    barrier = pltpu.get_barrier_semaphore()
-
-    def greet_group(d, carry):
-        pl.semaphore_signal(
-            barrier, inc=1, device_id=(base + (j + d) % 16, mode), device_id_type=MESH
-        )
-        return carry
-
-    for peer in modes:
-        pl.semaphore_signal(barrier, inc=1, device_id=(leaf, peer), device_id_type=MESH)
-    for peer in quarters:
-        for d in range(4):
-            pl.semaphore_signal(
-                barrier, inc=1, device_id=(peer * 16 + j, (mode + d) % 4), device_id_type=MESH
-            )
-    lax.fori_loop(1, 16, greet_group, 0)
     for load in loads[3:]:
         load.wait()
     own[0:8] = jnp.concatenate([sroot_ref[...] * SCALE, column(oroot_ref)], axis=1)
@@ -265,12 +263,8 @@
     omega = [wroot, wmid, wlow]
 
     def group_start(phase, src_of, dst):
-        def one(d, carry):
-            t = (j + d) % 16
+        for t in around:
             remote(src_of(t), dst, psend.at[phase], precv.at[phase], base + t, mode).start()
-            return carry
-
-        lax.fori_loop(1, 16, one, 0)
 
     def group_all(phase, landing):
         some = landing.at[pl.ds(0, 15)]
@@ -680,8 +674,10 @@
             gram_in(peer, (mode + d) % 4).wait_recv()
     for d in range(1, 4):
         gram_in(q, (mode + d) % 4).wait_recv()
-    for c in range(4):
-        gag[j, c] = (gc[c, 0] + gc[c, 1]) + (gc[c, 2] + gc[c, 3])
+    sums = [(gc[c, 0] + gc[c, 1]) + (gc[c, 2] + gc[c, 3]) for c in range(4)]
+    gag[j, 0] = sums[0]
+    gag[j, 1] = sums[1]
+    gag[j, 2] = jnp.where(low_lanes[0:8], pltpu.roll(sums[2], 64, 1), sums[3])
     group_start(19, lambda t: gag.at[j], gag.at[j])
     for d in range(4):
         for peer in (far0, far1):
@@ -734,7 +730,7 @@
         (128, 128),
         (16, 8, 128),
         (4, 4, 8, 128),
-        (16, 4, 8, 128),
+        (16, 3, 8, 128),
         (4, 56, 128),
         (8, 128),
         (16, 128),
@@ -748,7 +744,7 @@
     ]
     sems = [(11,), (6,), (3, 6), (3, 6), (20,), (20,), (3, 8), (3, 8), (10,), (10,)]
     sems += [(7, 4), (7, 4), (2, 3), (2, 3), (8, 4), (8, 4)]
-    shapes = [(16, 4, 8, 128), (4, 64, 512), (4, 56, 128), (8, 128), (16, 128), (32, 128)]
+    shapes = [(16, 3, 8, 128), (4, 64, 512), (4, 56, 128), (8, 128), (16, 128), (32, 128)]
     return pl.pallas_call(
         sweeps_kernel,
         out_shape=[jax.ShapeDtypeStruct(shape, F32) for shape in shapes],
@@ -838,16 +834,15 @@
         move.start()
     moves[0].wait()
     low_lanes = lax.broadcasted_iota(jnp.int32, (128, 128), 1) < 64
-    parts = [jnp.concatenate([gram_ref[t, c] for t in range(16)], axis=0) for c in range(4)]
-    turned = [pltpu.roll(part, 64, 1) for part in parts]
+    parts = [jnp.concatenate([gram_ref[t, c] for t in range(16)], axis=0) for c in range(3)]
+    turned = [pltpu.roll(parts[c], 64, 1) for c in range(2)]
+    first = jnp.where(low_lanes, parts[0], turned[1])
+    cross = jnp.where(low_lanes, turned[0], parts[1])
+    first = 0.5 * (first + first.T)
+    second = 0.5 * (parts[2] + parts[2].T)
     gram = jnp.concatenate(
-        [
-            jnp.concatenate([jnp.where(low_lanes, parts[c], turned[c + 1]) for c in (0, 2)], axis=1),
-            jnp.concatenate([jnp.where(low_lanes, turned[c], parts[c + 1]) for c in (0, 2)], axis=1),
-        ],
-        axis=0,
+        [jnp.concatenate([first, cross.T], axis=1), jnp.concatenate([cross, second], axis=1)], axis=0
     )
-    gram = 0.5 * (gram + gram.T)
     r = lax.broadcasted_iota(jnp.int32, (256, 256), 0)
     c = lax.broadcasted_iota(jnp.int32, (256, 256), 1)
     corner = jnp.where(r == c, gram, 0.0)
@@ -889,7 +884,7 @@
         in_specs=[hbm] * 6,
         out_specs=[vmem] * 4 + [hbm] * 3,
         scratch_shapes=[
-            pltpu.VMEM((16, 4, 8, 128), F32),
+            pltpu.VMEM((16, 3, 8, 128), F32),
             pltpu.VMEM((4, 64, 512), F32),
             pltpu.VMEM((4, 56, 128), F32),
             pltpu.VMEM((256, 512), F32),

time: 112 us -> 111 us (level)
  no operation moved by 1% of the time
where the time goes in v3:
time: 111 us
  Pallas kernels  110 us (99%)
    pallas_call x1, Pallas kernels, run_sweeps(): pl.pallas_call(sweeps_kernel, out_shape=[jax.ShapeDtypeStruct(shape, F32)...  100 us
    pallas_call x1, Pallas kernels, run_finish(): pl.pallas_call(finish_kernel, out_shape=[jax.ShapeDtypeStruct(shape, F32)...  10.1 us

profile of v3, /device:TPU:1, one launch (start us, length us, event | category | flops | bytes accessed | tf_op | source)
XLA Modules:
  0.0 111.2 jit_solution(17815471318359850402)
XLA Ops:
  0.6 100.3 %sweeps.1 = (f32[16,3,8,128]{3,2,1,0:T(8,128)}, f32[4,64,512]{2,1,0:T(8,128)}, f32[4,56,128]{2,1,0:T(8,128)}, f32[8,128]{1,0:T(8,128)}, f32[16,128]{1,0:T(8,128)}, /*index=5*/f32[32,128]{1,0:T(8,128)}) custom-call(s32[4]{0:T(128)} %sizes_ref.1, f32[1,512]{1,0:T(1,128)} %bitcast.13, f32[3,512,128]{2,1,0:T(8,128)} %coupling_ref.1, f32[64,512]{1,0:T(8,128)} %leaf_in.1, ...), custom_call_target="tpu_custom_call" | custom-call | tf_op jit(solution)/shard_map/sweeps/pallas_call | solution.py:748
  101.0 10.1 %finish.1 = (f32[64,512]{1,0:T(8,128)}, f32[8,64]{1,0:T(8,128)}, f32[16,64]{1,0:T(8,128)}, f32[32,64]{1,0:T(8,128)}, f32[8,128]{1,0:T(8,128)}, /*index=5*/f32[16,128]{1,0:T(8,128)}, f32[32,128]{1,0:T(8,128)}) custom-call(f32[16,3,8,128]{3,2,1,0:T(8,128)} %get-tuple-element.20.gram_in, f32[4,64,512]{2,1,0:T(8,128)} %get-tuple-element.21.next_in, ...), custom_call_target="tpu_custom_call" | custom-call | tf_op jit(solution)/shard_map/finish/pallas_call | solution.py:881

commit v4 on v3

--- a/solution.py
+++ b/solution.py
@@ -548,7 +548,7 @@
     for k in range(3):
         y_in(yl, 0, k).wait_recv()
         y_in(iy, 1, k).wait_recv()
-    blocks = [nt(yl[c], heavy) for c in range(4)]
+    leaf_part = nt(yl[...].reshape(256, 512), heavy * (1.0 / ROWS))
     results = [
         pltpu.make_async_copy(a, b, osem.at[n])
         for n, (a, b) in enumerate(
@@ -578,13 +578,11 @@
         )
         iface_ref[c] = (iy[c] - near) / weights
     results[1].start()
-    heavy_own = (iface_ref[mode] * weights)[:, 0:64].T
-    blocks = [
-        (blocks[c] + nt(iface_ref[c][:, 0:64].T, heavy_own)) * (1.0 / ROWS) for c in range(4)
-    ]
-    gp[...] = jnp.concatenate(
-        [jnp.concatenate(blocks[0:2], axis=0), jnp.concatenate(blocks[2:4], axis=0)], axis=1
-    )
+    heavy_own = (iface_ref[mode] * weights * (1.0 / ROWS))[:, 0:64].T
+    front = lax.broadcasted_iota(jnp.int32, (56, 128), 1) < 64
+    pairs = [jnp.where(front, iface_ref[c], pltpu.roll(iface_ref[c + 1], 64, 1)) for c in (0, 2)]
+    block = leaf_part + nt(jnp.concatenate(pairs, axis=1).T, heavy_own)
+    gp[...] = jnp.concatenate([block[0:128], block[128:256]], axis=1)
 
     def rows8(t):
         return pl.ds(pl.multiple_of(8 * t, 8), 8)

time: 111 us -> 112 us (level)
  no operation moved by 1% of the time
where the time goes in v4:
time: 112 us; the launch traced here: 111 us
  Pallas kernels  111 us (99%)
    pallas_call x1, Pallas kernels, run_sweeps(): pl.pallas_call(sweeps_kernel, out_shape=[jax.ShapeDtypeStruct(shape, F32)...  101 us
    pallas_call x1, Pallas kernels, run_finish(): pl.pallas_call(finish_kernel, out_shape=[jax.ShapeDtypeStruct(shape, F32)...  9.99 us

profile of v4, /device:TPU:1, one launch (start us, length us, event | category | flops | bytes accessed | tf_op | source)
XLA Modules:
  0.0 111.4 jit_solution(4654987918960173747)
XLA Ops:
  0.6 100.6 %sweeps.1 = (f32[16,3,8,128]{3,2,1,0:T(8,128)}, f32[4,64,512]{2,1,0:T(8,128)}, f32[4,56,128]{2,1,0:T(8,128)}, f32[8,128]{1,0:T(8,128)}, f32[16,128]{1,0:T(8,128)}, /*index=5*/f32[32,128]{1,0:T(8,128)}) custom-call(s32[4]{0:T(128)} %sizes_ref.1, f32[1,512]{1,0:T(1,128)} %bitcast.13, f32[3,512,128]{2,1,0:T(8,128)} %coupling_ref.1, f32[64,512]{1,0:T(8,128)} %leaf_in.1, ...), custom_call_target="tpu_custom_call" | custom-call | tf_op jit(solution)/shard_map/sweeps/pallas_call | solution.py:746
  101.3 10.0 %finish.1 = (f32[64,512]{1,0:T(8,128)}, f32[8,64]{1,0:T(8,128)}, f32[16,64]{1,0:T(8,128)}, f32[32,64]{1,0:T(8,128)}, f32[8,128]{1,0:T(8,128)}, /*index=5*/f32[16,128]{1,0:T(8,128)}, f32[32,128]{1,0:T(8,128)}) custom-call(f32[16,3,8,128]{3,2,1,0:T(8,128)} %get-tuple-element.20.gram_in, f32[4,64,512]{2,1,0:T(8,128)} %get-tuple-element.21.next_in, ...), custom_call_target="tpu_custom_call" | custom-call | tf_op jit(solution)/shard_map/finish/pallas_call | solution.py:879
